TPU v7x, 512 devices: a whole 4x4x16 slice. The times are simulated.
512 devices in a mesh: cuts: 2 (over y_lo), dp: 16 (over z), row: 4 (over y_hi, core), col: 4 (over x).
Axes of the slice: x: 4, y: 4 (y_hi: 2, y_lo: 2; y = y_hi * 2 + y_lo), z: 16, core: 2. Of those that a mesh axis runs over, the one named last changes fastest.
Arguments:
- tokens: bfloat16 [32768, 4096], P(('cuts', 'dp'), 'row'), may hold values from -6 to 6
- cotangent: bfloat16 [32768, 4096], P(('cuts', 'dp'), 'col'), may hold values from -0.03125 to 0.03125
- norm_gain: float32 [4096], P('row'), may hold values from 0.5 to 6
- row_prev: float32 [4, 1024], P('row', 'dp'), may hold values from 0.02 to 0.5
- col_prev: float32 [4096], P('col'), may hold values from 0.002 to 0.05
Outputs:
- update: float32 [4, 1024, 4096], P('row', 'dp', 'col')
- row_moment: float32 [4, 1024], P('row', 'dp')
- col_moment: float32 [4096], P('col')
All inputs are finite; a program needn't handle non-finite values.
Results may differ from a plain program's by a relative error of at most 0.0004.
Values sent between devices are 32-bit elements; how exact they have to be, the bound alone decides.
A program may use at most 64 MiB of HBM per device.

v0:
```python
import jax
import jax.numpy as jnp
from jax import lax
from jax.sharding import PartitionSpec as P

D = 4096
F = 4096
decay_rate = 0.975
epsilon_one = 1e-30
clip_level = 1.0


def gradient_rows(inputs, cotangent, gains):
    product = lax.dot_general(
        inputs, cotangent, (((0,), (0,)), ((), ())), preferred_element_type=jnp.float32
    )
    return product * gains[:, None]


def adafactor_step(gradient, rows_prev, cols_prev, down_columns, all_total):
    squares = gradient * gradient
    row_sum = lax.psum(jnp.sum(squares, axis=1), "col")
    col_sum = down_columns(jnp.sum(squares, axis=0))
    row_moment = decay_rate * rows_prev + (1.0 - decay_rate) * (row_sum / F + epsilon_one)
    col_moment = decay_rate * cols_prev + (1.0 - decay_rate) * (col_sum / D + epsilon_one)
    factor = row_moment[:, None] * col_moment[None, :]
    raw_update = gradient / jnp.sqrt(factor)
    total_squares = all_total(jnp.sum(raw_update * raw_update))
    clip_scale = jnp.maximum(1.0, jnp.sqrt(total_squares / (D * F)) / clip_level)
    return (raw_update / clip_scale, row_moment, col_moment)


def body(tokens, cotangent, norm_gain, row_prev, col_prev):
    slice_part = lax.psum_scatter(
        gradient_rows(tokens, cotangent, norm_gain), "dp", scatter_dimension=0, tiled=True
    )
    gradient = lax.psum(slice_part, "cuts")
    update, row_moment, col_moment = adafactor_step(
        gradient,
        row_prev[0],
        col_prev,
        lambda values: lax.psum(values, ("dp", "row")),
        lambda values: lax.psum(values, ("dp", "row", "col")),
    )
    return (update[None], row_moment[None], col_moment)


def solution(mesh):
    return jax.shard_map(
        body,
        mesh=mesh,
        in_specs=(
            P(("cuts", "dp"), "row"),
            P(("cuts", "dp"), "col"),
            P("row"),
            P("row", "dp"),
            P("col"),
        ),
        out_specs=(P("row", "dp", "col"), P("row", "dp"), P("col")),
        check_vma=False,
    )
```

profile of v0, /device:TPU:2, one launch (start us, length us, event | category | flops | bytes accessed | tf_op | source)
XLA Modules:
  0.0 946.8 jit_solution(15512773143829418762)
XLA Ops:
  7.2 0.0 copy-start
  7.2 0.0 reduce-scatter.2.cloned.1.call-start
  7.2 1.5 copy-done
  8.8 5.9 convolution_multiply_fusion
  14.7 0.0 copy-start.4
  14.7 0.0 copy-start.2
  14.7 0.0 reduce-scatter.2.cloned.1.call-update
  14.7 0.0 all-reduce.2.cloned.1.call-start
  14.7 84.2 %reduce-scatter.2.cloned.1.call-done = f32[64,1024]{1,0:T(8,128)} async-done(((f32[1024,1024]{1,0:T(8,128)}), f32[64,1024]{1,0:T(8,128)}) %reduce-scatter.2.cloned.1.call-update) | async-done | bytes 262160 | tf_op jit(solution)/shard_map/reduce_scatter | solution.py:34
  99.0 0.0 all-reduce.2.cloned.1.call-update
  99.0 45.7 %all-reduce.2.cloned.1.call-done = f32[64,1024]{1,0:T(8,128)} async-done(((f32[64,1024]{1,0:T(8,128)}), f32[64,1024]{1,0:T(8,128)}) %all-reduce.2.cloned.1.call-update) | async-done | bytes 262160 | tf_op jit(solution)/shard_map/psum | solution.py:37
  144.7 1.1 multiply_reduce_fusion.2
  145.8 8.6 psum.29
  154.4 132.2 %psum.30 = f32[1024]{0:T(1024)S(1)} all-reduce(f32[1024]{0:T(1024)S(1)} %get-tuple-element.4), channel_id=1, replica_groups=mesh['cuts'=2,'dp'=16,'row'=4,'col'=4] {'dp','row'}, use_global_device_ids=true, to_apply=%region_5.0 | all-reduce | flops 1024 | bytes 8192 | tf_op jit(solution)/shard_map/psum | solution.py:42
  286.6 0.0 copy-done.4
  286.6 0.0 copy-done.2
  286.6 0.0 copy-start.3
  286.7 0.0 copy-start.1
  286.7 1.7 multiply_reduce_fusion
  288.4 649.1 %psum.31 = f32[]{:T(128)} all-reduce(f32[]{:T(128)} %multiply_reduce_fusion), channel_id=1, replica_groups=mesh['cuts'=2,'dp'=16,'row'=4,'col'=4] {'dp','row','col'}, use_global_device_ids=true, to_apply=%region_7.0 | all-reduce | flops 1 | bytes 8 | tf_op jit(solution)/shard_map/psum | solution.py:43
  938.2 1.8 divide_bitcast_fusion
  939.9 0.0 copy-done.3
  939.9 0.0 copy-done.1
  (2 shorter events, 0.0 us)
Async XLA Ops:
  7.2 1.6 copy-start
  7.2 91.8 %reduce-scatter.2.cloned.1.call-start = ((), (), s32[]{:S(2)}) async-start(), calls=%async_computation.1 | async-start | bytes 4456448 | tf_op jit(solution)/shard_map/reduce_scatter | solution.py:34
  14.7 272.0 %copy-start.4 = (f32[1,64]{1,0:T(1,128)S(1)}, f32[1,64]{1,0:T(1,128)}, u32[]{:S(2)}) copy-start(f32[1,64]{1,0:T(1,128)} %param.8) | copy-start | bytes 772
  14.7 272.0 %copy-start.2 = (f32[1024]{0:T(1024)S(1)}, f32[1024]{0:T(1024)}, u32[]{:S(2)}) copy-start(f32[1024]{0:T(1024)} %param.9) | copy-start | bytes 12292
  14.7 130.0 %all-reduce.2.cloned.1.call-start = ((), (), s32[]{:S(2)}) async-start(), calls=%async_computation.2 | async-start | bytes 524288 | tf_op jit(solution)/shard_map/psum | solution.py:37
  286.6 653.3 %copy-start.3 = (f32[64]{0:T(128)}, f32[64]{0:T(128)S(1)}, u32[]{:S(2)}) copy-start(f32[64]{0:T(128)S(1)} %bitcast_add_fusion) | copy-start | bytes 772
  286.7 653.3 %copy-start.1 = (f32[1024]{0:T(1024)}, f32[1024]{0:T(1024)S(1)}, u32[]{:S(2)}) copy-start(f32[1024]{0:T(1024)S(1)} %multiply_add_fusion) | copy-start | bytes 12292
Sparse Core Ops, SparseCore 0:
  14.8 84.1 reduce-scatter.1
  101.8 42.8 all-reduce.1
where the time goes:
time: 947 us
  blocking collectives  790 us (83%)
  waiting for transfers between devices  130 us (14%)
  between operations  14.8 us (2%)
    psum x1, blocking collectives, body(): lax.psum(values, ('dp', 'row', 'col'))  649 us
    psum x1, blocking collectives, body(): lax.psum(values, ('dp', 'row'))  132 us
    reduce_scatter x1, waiting for transfers between devices, body(): lax.psum_scatter(gradient_rows(tokens, cotangent, norm_gain), 'dp', scatt...  84.2 us
    psum x1, waiting for transfers between devices, body(): gradient = lax.psum(slice_part, 'cuts')  45.7 us
  transfers between devices with their start and end apart: 2, of which 2 were waited for; matrix products, arithmetic and copies ran while one was open for 0% of the time, Pallas kernels for 0%

commit v1 on v0

--- a/solution.py
+++ b/solution.py
@@ -35,11 +35,12 @@
         gradient_rows(tokens, cotangent, norm_gain), "dp", scatter_dimension=0, tiled=True
     )
     gradient = lax.psum(slice_part, "cuts")
+    return_all_lines = lambda in_array: lax.psum(lax.psum(in_array, "dp"), "row")
     update, row_moment, col_moment = adafactor_step(
         gradient,
         row_prev[0],
         col_prev,
-        lambda values: lax.psum(values, ("dp", "row")),
+        lambda values: return_all_lines(values),
         lambda values: lax.psum(values, ("dp", "row", "col")),
     )
     return (update[None], row_moment[None], col_moment)

time: 947 us -> 854 us (0.902)
  the two profiles are of different devices: /device:TPU:2 before, /device:TPU:8 now
where the time goes in v1:
time: 854 us; the launch traced here: 853 us
  blocking collectives  696 us (81%)
  waiting for transfers between devices  130 us (15%)
  between operations  14.8 us (2%)
    psum x1, blocking collectives, body(): lax.psum(values, ('dp', 'row', 'col'))  649 us
    reduce_scatter x1, waiting for transfers between devices, body(): lax.psum_scatter(gradient_rows(tokens, cotangent, norm_gain), 'dp', scatt...  84.3 us
    psum x1, waiting for transfers between devices, body(): gradient = lax.psum(slice_part, 'cuts')  45.6 us
    psum x1, blocking collectives, body(): lax.psum(in_array, 'dp')  31.3 us
  transfers between devices with their start and end apart: 2, of which 2 were waited for; matrix products, arithmetic and copies ran while one was open for 0% of the time, Pallas kernels for 0%

profile of v1, /device:TPU:8, one launch (start us, length us, event | category | flops | bytes accessed | tf_op | source)
XLA Modules:
  0.0 853.3 jit_solution(3671826420791679896)
XLA Ops:
  7.2 0.0 copy-start
  7.2 0.0 reduce-scatter.2.cloned.1.call-start
  7.2 1.5 copy-done
  8.8 5.9 convolution_multiply_fusion
  14.7 0.0 copy-start.4
  14.7 0.0 copy-start.2
  14.7 0.0 reduce-scatter.2.cloned.1.call-update
  14.7 0.0 all-reduce.2.cloned.1.call-start
  14.7 84.3 %reduce-scatter.2.cloned.1.call-done = f32[64,1024]{1,0:T(8,128)} async-done(((f32[1024,1024]{1,0:T(8,128)}), f32[64,1024]{1,0:T(8,128)}) %reduce-scatter.2.cloned.1.call-update) | async-done | bytes 262160 | tf_op jit(solution)/shard_map/reduce_scatter | solution.py:34
  99.0 0.0 all-reduce.2.cloned.1.call-update
  99.1 45.6 %all-reduce.2.cloned.1.call-done = f32[64,1024]{1,0:T(8,128)} async-done(((f32[64,1024]{1,0:T(8,128)}), f32[64,1024]{1,0:T(8,128)}) %all-reduce.2.cloned.1.call-update) | async-done | bytes 262160 | tf_op jit(solution)/shard_map/psum | solution.py:37
  144.7 1.1 multiply_reduce_fusion.2
  145.8 9.4 %psum.36 = f32[64]{0:T(128)S(1)} all-reduce(f32[64]{0:T(128)S(1)} %get-tuple-element.3), channel_id=1, replica_groups=mesh['cuts'=2,'dp'=16,'row'=4,'col'=4] {'col'}, use_global_device_ids=true, to_apply=%region_3.0 | all-reduce | flops 64 | bytes 512 | tf_op jit(solution)/shard_map/psum | solution.py:22
  155.2 31.3 %psum.37 = f32[1024]{0:T(1024)S(1)} all-reduce(f32[1024]{0:T(1024)S(1)} %get-tuple-element.4), channel_id=1, replica_groups=mesh['cuts'=2,'dp'=16,'row'=4,'col'=4] {'dp'}, use_global_device_ids=true, to_apply=%region_5.0 | all-reduce | flops 1024 | bytes 8192 | tf_op jit(solution)/shard_map/psum | solution.py:38
  186.5 7.2 psum.38
  193.7 0.0 copy-done.4
  193.7 0.0 copy-done.2
  193.7 0.0 copy-start.3
  193.7 0.0 copy-start.1
  193.7 1.7 multiply_reduce_fusion
  195.4 648.6 %psum.39 = f32[]{:T(128)} all-reduce(f32[]{:T(128)} %multiply_reduce_fusion), channel_id=1, replica_groups=mesh['cuts'=2,'dp'=16,'row'=4,'col'=4] {'dp','row','col'}, use_global_device_ids=true, to_apply=%region_8.0 | all-reduce | flops 1 | bytes 8 | tf_op jit(solution)/shard_map/psum | solution.py:44
  844.7 1.8 divide_bitcast_fusion
  846.5 0.0 copy-done.3
  846.5 0.0 copy-done.1
  (2 shorter events, 0.0 us)
Async XLA Ops:
  7.2 1.6 copy-start
  7.2 91.9 %reduce-scatter.2.cloned.1.call-start = ((), (), s32[]{:S(2)}) async-start(), calls=%async_computation.1 | async-start | bytes 4456448 | tf_op jit(solution)/shard_map/reduce_scatter | solution.py:34
  14.7 179.0 %copy-start.4 = (f32[1,64]{1,0:T(1,128)S(1)}, f32[1,64]{1,0:T(1,128)}, u32[]{:S(2)}) copy-start(f32[1,64]{1,0:T(1,128)} %param.8) | copy-start | bytes 772
  14.7 179.0 %copy-start.2 = (f32[1024]{0:T(1024)S(1)}, f32[1024]{0:T(1024)}, u32[]{:S(2)}) copy-start(f32[1024]{0:T(1024)} %param.9) | copy-start | bytes 12292
  14.7 130.0 %all-reduce.2.cloned.1.call-start = ((), (), s32[]{:S(2)}) async-start(), calls=%async_computation.2 | async-start | bytes 524288 | tf_op jit(solution)/shard_map/psum | solution.py:37
  193.7 652.8 %copy-start.3 = (f32[64]{0:T(128)}, f32[64]{0:T(128)S(1)}, u32[]{:S(2)}) copy-start(f32[64]{0:T(128)S(1)} %bitcast_add_fusion) | copy-start | bytes 772
  193.7 652.8 %copy-start.1 = (f32[1024]{0:T(1024)}, f32[1024]{0:T(1024)S(1)}, u32[]{:S(2)}) copy-start(f32[1024]{0:T(1024)S(1)} %multiply_add_fusion) | copy-start | bytes 12292
Sparse Core Ops, SparseCore 0:
  14.8 84.1 reduce-scatter.1
  101.9 42.7 all-reduce.1
